TPU v7x, 32 devices: a whole 2x2x4 slice. The times are simulated.
32 devices in a mesh: section: 4 (over z), seq: 8 (over y, x, core).
Axes of the slice: x: 2, y: 2, z: 4, core: 2. Of those that a mesh axis runs over, the one named last changes fastest.
Arguments:
- inputs: bfloat16 [512, 4096], P('seq'), may hold values from -6 to 6
- gains: float32 [4, 4096], P('section'), may hold values from 0.25 to 1.75
- weights: bfloat16 [4, 4096, 4096], P('section', None, 'seq'), may hold values from -0.125 to 0.125
- keep: int32 [4, 64, 64], P('section', None, 'seq'), may hold values 0 or 1
- cotangent: bfloat16 [512, 4096], P('seq'), may hold values from -6 to 6
Outputs:
- layer_outputs: bfloat16 [4, 512, 4096], P('section', 'seq')
- layer_grads: bfloat16 [4, 512, 4096], P('section', 'seq')
- weight_grads: bfloat16 [4, 4096, 4096], P('section', None, 'seq')
- gain_grads: float32 [4, 4096], P('section', 'seq')
Inputs may be any that keep to these rules, and one draw needn't show every extreme that they name: `keep`: 1 keeps a 64 x 64 block of the projection, 0 prunes it.
All inputs are finite; a program needn't handle non-finite values.
Results may differ from a plain program's by a relative error of at most 0.018.
Values may be sent and summed in bfloat16 or wider, within the bound.
A program may use at most 64 MiB of HBM per device.

v0:
```python
import functools

import jax
import jax.numpy as jnp
from jax import lax
from jax.experimental import pallas as pl
from jax.experimental.pallas import tpu as pltpu
from jax.sharding import PartitionSpec as P

EPS = 1e-05
ROWS = 16
F32 = jnp.float32
BF16 = jnp.bfloat16


def dot(a, b, dims):
    return lax.dot_general(a, b, (dims, ((), ())), preferred_element_type=F32)


def to_row(column, rows):
    n = column.shape[0]
    return jnp.transpose(jnp.broadcast_to(column, (n, 128)))[:rows]


def to_col(row):
    n = row.shape[1]
    return jnp.transpose(jnp.broadcast_to(row, (128, n)))[:, :1]


def kernel(
    L, S, M, block,
    x_ref, gain_ref, w_ref, keep_ref, cot_ref,
    lo_ref, lg_ref, wg_ref, gg_ref,
    A, wp, raw, inv_ref, zout, g, zg, gs, tot, psend, prec, qsend, qrec, nsend, nrec, ggs, ggr,
    in_sem, cot_sem, ag_sem, lo2_sem, n_sem, p_sem, q_sem, lg_sem, gg_sem, zf_sem, lo_sem, zb_sem,
):
    r = x_ref.shape[1]
    D = w_ref.shape[0]
    C = w_ref.shape[1]
    MB = S * r
    H = S // 2
    sec = lax.axis_index("section")
    me = lax.axis_index("seq")
    pair = me // 2
    par = me % 2
    partner = pair * 2 + 1 - par
    is_first = sec == 0
    is_last = sec == L - 1

    def col(i):
        return pl.ds(pl.multiple_of(i * C, C), C)

    def rows(i):
        return pl.ds(pl.multiple_of(i * r, r), r)

    def to(j):
        return (me + j) % S

    def fr(j):
        return (me + S - j) % S

    def mate_to(j):
        return ((pair + j) % H) * 2 + par

    def mate_fr(j):
        return ((pair + H - j) % H) * 2 + par

    def cp(src, dst, sem, idx, dev, section=None):
        return pltpu.make_async_remote_copy(
            src_ref=src,
            dst_ref=dst,
            send_sem=sem.at[(0,) + idx],
            recv_sem=sem.at[(1,) + idx],
            device_id=(sec if section is None else section, dev),
            device_id_type=pl.DeviceIdType.MESH,
        )

    def same(ref, sem, idx, dev, section=None):
        return cp(ref, ref, sem, idx, dev, section)

    def in_tx(m, j):
        d = to(j)
        return cp(x_ref.at[m, :, col(d)], A.at[m, rows(me), col(d)], in_sem, (m, j), d)

    def in_rx(m, j):
        f = fr(j)
        return same(A.at[m, rows(f), col(me)], in_sem, (m, j), f)

    def cot_tx(m, j):
        d = to(j)
        return cp(cot_ref.at[m, :, col(d)], g.at[m, rows(me), :], cot_sem, (m, j), d)

    def cot_rx(m, j):
        f = fr(j)
        return same(g.at[m, rows(f), :], cot_sem, (m, j), f)

    def ag_tx(m, j):
        return same(A.at[m, :, col(me)], ag_sem, (m, j), mate_to(j))

    def ag_rx(m, j):
        f = mate_fr(j)
        return same(A.at[m, :, col(f)], ag_sem, (m, j), f)

    def ag_ptx(m):
        return same(A.at[m, :, col(me)], ag_sem, (m, 0), partner)

    def ag_prx(m):
        return same(A.at[m, :, col(partner)], ag_sem, (m, 0), partner)

    def ag_ftx(m, j):
        return same(A.at[m, :, col(mate_fr(j))], ag_sem, (m, H + j), partner)

    def ag_frx(m, j):
        b = mate_fr(j) + 1 - 2 * par
        return same(A.at[m, :, col(b)], ag_sem, (m, H + j), partner)

    def zf_tx(m):
        return cp(zout.at[m], A.at[m, :, col(me)], zf_sem, (m,), me, sec + 1)

    def zf_rx(m):
        return same(A.at[m, :, col(me)], zf_sem, (m,), me, sec - 1)

    def lo_tx(m):
        return cp(A.at[m, rows(me), :], lo_ref.at[m], lo_sem, (m,), me, sec - 1)

    def lo_rx(m):
        return same(lo_ref.at[m], lo_sem, (m,), me, sec + 1)

    def lo2_tx(m, j):
        d = to(j)
        return cp(zout.at[m, rows(d), :], lo_ref.at[m, :, col(me)], lo2_sem, (m, j), d)

    def lo2_rx(m, j):
        f = fr(j)
        return same(lo_ref.at[m, :, col(f)], lo2_sem, (m, j), f)

    def n_tx(m, j):
        return cp(nsend.at[m], nrec.at[m, j], n_sem, (m, j), to(j))

    def n_rx(m, j):
        return same(nrec.at[m, j], n_sem, (m, j), fr(j))

    def p_tx(m, j):
        return cp(psend.at[m, j], prec.at[m, j], p_sem, (m, j), partner)

    def p_rx(m, j):
        return same(prec.at[m, j], p_sem, (m, j), partner)

    def q_tx(m, j):
        return cp(qsend.at[m, j], qrec.at[m, j], q_sem, (m, j), mate_to(j))

    def q_rx(m, j):
        return same(qrec.at[m, j], q_sem, (m, j), mate_fr(j))

    def zb_tx(m):
        return cp(zg.at[m], g.at[m], zb_sem, (m,), me, sec - 1)

    def zb_rx(m):
        return same(g.at[m], zb_sem, (m,), me, sec + 1)

    def lg_tx(m, j):
        d = to(j)
        return cp(zg.at[m, rows(d), :], lg_ref.at[m, :, col(me)], lg_sem, (m, j), d)

    def lg_rx(m, j):
        f = fr(j)
        return same(lg_ref.at[m, :, col(f)], lg_sem, (m, j), f)

    def gg_tx(j):
        d = to(j)
        return cp(ggs.at[d], ggr.at[j], gg_sem, (j,), d)

    def gg_rx(j):
        return same(ggr.at[j], gg_sem, (j,), fr(j))

    others = range(1, S)
    mates = range(1, H)

    barrier = pltpu.get_barrier_semaphore()

    def greet(section, seq):
        pl.semaphore_signal(
            barrier, inc=1, device_id=(section, seq), device_id_type=pl.DeviceIdType.MESH
        )

    for j in others:
        greet(sec, to(j))

    @pl.when(sec > 0)
    def _():
        greet(sec - 1, me)

    @pl.when(sec < L - 1)
    def _():
        greet(sec + 1, me)

    neighbours = jnp.minimum(sec, 1) + jnp.minimum(L - 1 - sec, 1)
    pl.semaphore_wait(barrier, S - 1 + neighbours)

    @pl.when(is_first)
    def _():
        @pl.loop(0, M)
        def _(m):
            for j in others:
                in_tx(m, j).start()
            A[m, rows(me), col(me)] = x_ref[m, :, col(me)]

    @pl.when(is_last)
    def _():
        @pl.loop(0, M)
        def _(m):
            for j in others:
                cot_tx(m, j).start()
            g[m, rows(me), :] = cot_ref[m, :, col(me)]

    def keep_of(b):
        return jnp.broadcast_to(keep_ref[b][:, None, :], (C // block, block, C)).reshape(C, C)

    @pl.loop(0, S)
    def _(b):
        gain = to_col(gain_ref[:, col(b)])
        wp[col(b), :] = (w_ref[col(b), :].astype(F32) * gain * keep_of(b)).astype(BF16)

    def gather_start(m):
        for j in mates:
            ag_tx(m, j).start()
        ag_ptx(m).start()

    @pl.when(is_first)
    def _():
        @pl.loop(0, M)
        def _(m):
            for j in others:
                in_rx(m, j).wait_recv()
            gather_start(m)

    @pl.loop(0, M)
    def _(m):
        @pl.when(sec > 0)
        def _():
            zf_rx(m).wait_recv()
            gather_start(m)

        for j in mates:
            ag_rx(m, j).wait_recv()
            ag_ftx(m, j).start()
        ag_prx(m).wait_recv()
        for j in mates:
            ag_frx(m, j).wait_recv()

        @pl.when(sec > 0)
        def _():
            lo_tx(m).start()

        acc = jnp.zeros((MB, C), F32)
        squares = jnp.zeros((MB, 1), F32)
        for b in range(S):
            part = A[m, :, b * C:(b + 1) * C]
            acc = acc + dot(part, wp[b * C:(b + 1) * C, :], ((1,), (0,)))
            wide = part.astype(F32)
            squares = squares + jnp.sum(wide * wide, axis=1, keepdims=True)
        inv = lax.rsqrt(squares / D + EPS)
        raw[m] = acc
        inv_ref[m] = jnp.broadcast_to(inv, (MB, 128))
        zout[m] = (A[m, :, col(me)].astype(F32) + inv * acc).astype(BF16)

        @pl.when(sec < L - 1)
        def _():
            zf_tx(m).start()

        @pl.when(is_last)
        def _():
            for j in others:
                lo2_tx(m, j).start()
            lo_ref[m, :, col(me)] = zout[m, rows(me), :]

    def weight_grads():
        @pl.loop(0, S)
        def _(b):
            left = A[:, :, col(b)].reshape(M * MB, C)
            right = gs[...].reshape(M * MB, C)
            u = dot(left, right, ((0,), (0,))) * keep_of(b)
            wg_ref[col(b), :] = (u * to_col(gain_ref[:, col(b)])).astype(BF16)
            total = jnp.sum(u * w_ref[col(b), :].astype(F32), axis=1, keepdims=True)
            ggs[b] = to_row(total, 8)

        for j in others:
            gg_tx(j).start()

    @pl.loop(0, M)
    def _(m):
        @pl.when(is_last)
        def _():
            for j in others:
                cot_rx(m, j).wait_recv()

        @pl.when(sec < L - 1)
        def _():
            zb_rx(m).wait_recv()

        def partial_of(b):
            return dot(g[m], wp[col(b), :], ((1,), (1,)))

        order = list(mates) + [0]
        for j in order:
            psend[m, j] = partial_of(((pair + j) % H) * 2 + 1 - par).astype(BF16)
            p_tx(m, j).start()
        inv = inv_ref[m][:, :1]
        gv = g[m].astype(F32)
        nsend[m] = to_row(jnp.sum(gv * raw[m], axis=1, keepdims=True), 8)
        for j in others:
            n_tx(m, j).start()
        gs[m] = (gv * inv).astype(BF16)
        for j in mates:
            mine = partial_of(mate_to(j))
            p_rx(m, j).wait_recv()
            qsend[m, j] = (mine + prec[m, j].astype(F32)).astype(BF16)
            q_tx(m, j).start()
        tot[...] = partial_of(me)

        @pl.when(m == M - 1)
        def _():
            weight_grads()

        p_rx(m, 0).wait_recv()
        for j in mates:
            q_rx(m, j).wait_recv()
        for j in others:
            n_rx(m, j).wait_recv()
        scaled = tot[...] + prec[m, 0].astype(F32)
        for j in mates:
            scaled = scaled + qrec[m, j].astype(F32)
        sums = nsend[m]
        for j in others:
            sums = sums + nrec[m, j]
        inner = to_col(sums[:1]) / D
        grad = (
            g[m].astype(F32)
            + inv * scaled
            - A[m, :, col(me)].astype(F32) * (inv * inv * inv * inner)
        )
        zg[m] = grad.astype(BF16)

        @pl.when(sec > 0)
        def _():
            zb_tx(m).start()

        for j in others:
            lg_tx(m, j).start()
        lg_ref[m, :, col(me)] = zg[m, rows(me), :]

    for j in others:
        gg_rx(j).wait_recv()
    sums = ggs[me]
    for j in others:
        sums = sums + ggr[j]
    gg_ref[...] = sums[:1]

    for j in others:
        gg_tx(j).wait_send()

    @pl.loop(0, M)
    def _(m):
        @pl.when(is_first)
        def _():
            for j in others:
                in_tx(m, j).wait_send()

        @pl.when(is_last)
        def _():
            for j in others:
                cot_tx(m, j).wait_send()
                lo2_tx(m, j).wait_send()
                lo2_rx(m, j).wait_recv()

        @pl.when(sec < L - 1)
        def _():
            zf_tx(m).wait_send()
            lo_rx(m).wait_recv()

        @pl.when(sec > 0)
        def _():
            lo_tx(m).wait_send()
            zb_tx(m).wait_send()

        for j in mates:
            ag_tx(m, j).wait_send()
            ag_ftx(m, j).wait_send()
            q_tx(m, j).wait_send()
        ag_ptx(m).wait_send()
        for j in range(H):
            p_tx(m, j).wait_send()
        for j in others:
            n_tx(m, j).wait_send()
            lg_tx(m, j).wait_send()
            lg_rx(m, j).wait_recv()


def local(L, S, inputs, gains, weights, keep, cotangent):
    rows_dev, D = inputs.shape
    C = weights.shape[2]
    r = ROWS
    M = rows_dev // r
    MB = S * r
    H = S // 2
    block = D // keep.shape[1]
    keep_cols = jnp.repeat(keep[0].astype(F32), block, axis=1).reshape(S, C // block, C)
    vmem = pl.BlockSpec(memory_space=pltpu.VMEM)
    dma = pltpu.SemaphoreType.DMA
    lo, lg, wg, gg = pl.pallas_call(
        functools.partial(kernel, L, S, M, block),
        out_shape=(
            jax.ShapeDtypeStruct((M, r, D), BF16),
            jax.ShapeDtypeStruct((M, r, D), BF16),
            jax.ShapeDtypeStruct((D, C), BF16),
            jax.ShapeDtypeStruct((1, C), F32),
        ),
        in_specs=[vmem] * 5,
        out_specs=(vmem,) * 4,
        scratch_shapes=[
            pltpu.VMEM((M, MB, D), BF16),
            pltpu.VMEM((D, C), BF16),
            pltpu.VMEM((M, MB, C), F32),
            pltpu.VMEM((M, MB, 128), F32),
            pltpu.VMEM((M, MB, C), BF16),
            pltpu.VMEM((M, MB, C), BF16),
            pltpu.VMEM((M, MB, C), BF16),
            pltpu.VMEM((M, MB, C), BF16),
            pltpu.VMEM((MB, C), F32),
            pltpu.VMEM((M, H, MB, C), BF16),
            pltpu.VMEM((M, H, MB, C), BF16),
            pltpu.VMEM((M, H, MB, C), BF16),
            pltpu.VMEM((M, H, MB, C), BF16),
            pltpu.VMEM((M, 8, MB), F32),
            pltpu.VMEM((M, S, 8, MB), F32),
            pltpu.VMEM((S, 8, C), F32),
            pltpu.VMEM((S, 8, C), F32),
            dma((2, M, S)),
            dma((2, M, S)),
            dma((2, M, S)),
            dma((2, M, S)),
            dma((2, M, S)),
            dma((2, M, H)),
            dma((2, M, H)),
            dma((2, M, S)),
            dma((2, S)),
            dma((2, M)),
            dma((2, M)),
            dma((2, M)),
        ],
        compiler_params=pltpu.CompilerParams(
            collective_id=0, has_side_effects=True, vmem_limit_bytes=60 * 1024 * 1024
        ),
        cost_estimate=pl.CostEstimate(
            flops=6 * M * MB * D * C, bytes_accessed=12 * D * C, transcendentals=0
        ),
    )(
        inputs.reshape(M, r, D),
        gains,
        weights[0],
        keep_cols,
        cotangent.reshape(M, r, D),
    )
    return (
        lo.reshape(1, rows_dev, D),
        lg.reshape(1, rows_dev, D),
        wg[None],
        gg,
    )


def solution(mesh):
    placed = (
        P("seq", None),
        P("section", None),
        P("section", None, "seq"),
        P("section", None, "seq"),
        P("seq", None),
    )
    return jax.shard_map(
        functools.partial(local, mesh.shape["section"], mesh.shape["seq"]),
        mesh=mesh,
        in_specs=placed,
        out_specs=(
            P("section", "seq", None),
            P("section", "seq", None),
            P("section", None, "seq"),
            P("section", "seq"),
        ),
        check_vma=False,
    )
```

profile of v0, /device:TPU:0, one launch (start us, length us, event | category | flops | bytes accessed | tf_op | source)
XLA Modules:
  0.0 205.3 jit_solution(11829907912231566971)
XLA Ops:
  0.6 0.7 convert_bitcast_fusion
  1.3 0.1 copy.9
  1.4 0.1 broadcast_in_dim.6
  1.5 0.8 reshape_reshape.3.keep_ref
  2.3 194.2 %shard_map.84 = (bf16[4,16,4096]{2,1,0:T(8,128)(2,1)}, bf16[4,16,4096]{2,1,0:T(8,128)(2,1)}, bf16[4096,512]{1,0:T(8,128)(2,1)}, f32[1,512]{1,0:T(1,128)}) custom-call(bf16[4,16,4096]{2,1,0:T(8,128)(2,1)} %bitcast.12, f32[1,4096]{1,0:T(1,128)} %gain_ref.1, bf16[4096,512]{1,0:T(8,128)(2,1)} %bitcast.11, f32[8,8,512]{2,1,0:T(8,128)} %reshape_reshape.3.keep_ref, ...), custom_call_target="tpu_custom_call" | custom-call | flops 6442450944 | bytes 25165824 | tf_op jit(solution)/shard_map/pallas_call | solution.py:410
  196.5 1.9 copy.14
  198.3 1.9 copy.15
  200.2 0.0 copy-start
  200.2 4.5 %copy.16 = bf16[1,4096,512]{2,1,0:T(8,128)(2,1)} copy(bf16[1,4096,512]{2,1,0:T(8,128)(2,1)} %bitcast.8) | data formatting | bytes 8388608
  204.7 0.0 copy-done
  204.7 0.6 copy.17
Async XLA Ops:
  200.2 4.5 %copy-start = (f32[1,512]{1,0:T(1,128)S(1)}, f32[1,512]{1,0:T(1,128)}, u32[]{:S(2)}) copy-start(f32[1,512]{1,0:T(1,128)} %get-tuple-element.19) | copy-start | bytes 6148
where the time goes:
time: 206 us; the launch traced here: 205 us
  Pallas kernels  194 us (94%)
  local copies, waits for them, and re-layouts  9.77 us (5%)
    pallas_call x1, Pallas kernels, local(): pl.pallas_call(functools.partial(kernel, L, S, M, block), out_shape=(jax....  194 us
    unnamed x6, local copies, waits for them, and re-layouts  8.79 us

commit v1 on v0

--- a/solution.py
+++ b/solution.py
@@ -32,7 +32,7 @@
     x_ref, gain_ref, w_ref, keep_ref, cot_ref,
     lo_ref, lg_ref, wg_ref, gg_ref,
     A, wp, raw, inv_ref, zout, g, zg, gs, tot, psend, prec, qsend, qrec, nsend, nrec, ggs, ggr,
-    in_sem, cot_sem, ag_sem, lo2_sem, n_sem, p_sem, q_sem, lg_sem, gg_sem, zf_sem, lo_sem, zb_sem,
+    cot_sem, ag_sem, lo2_sem, n_sem, p_sem, q_sem, lg_sem, gg_sem, zf_sem, lo_sem, zb_sem,
 ):
     r = x_ref.shape[1]
     D = w_ref.shape[0]
@@ -59,11 +59,21 @@
     def fr(j):
         return (me + S - j) % S
 
-    def mate_to(j):
-        return ((pair + j) % H) * 2 + par
-
-    def mate_fr(j):
-        return ((pair + H - j) % H) * 2 + par
+    def mate(k):
+        other, bit = pair, 1
+        while bit < H:
+            if k & bit:
+                other = other + bit - 2 * bit * ((other // bit) % 2)
+            bit *= 2
+        return other * 2 + par
+
+    relayed = H == 4
+    direct = (1, 2) if relayed else tuple(range(1, H))
+    near = 1 + par
+    far = 2 - par
+
+    def mate_of(k):
+        return mate(1) * (2 - k) + mate(2) * (k - 1)
 
     def cp(src, dst, sem, idx, dev, section=None):
         return pltpu.make_async_remote_copy(
@@ -78,13 +88,8 @@
     def same(ref, sem, idx, dev, section=None):
         return cp(ref, ref, sem, idx, dev, section)
 
-    def in_tx(m, j):
-        d = to(j)
-        return cp(x_ref.at[m, :, col(d)], A.at[m, rows(me), col(d)], in_sem, (m, j), d)
-
-    def in_rx(m, j):
-        f = fr(j)
-        return same(A.at[m, rows(f), col(me)], in_sem, (m, j), f)
+    others = range(1, S)
+    mates = range(1, H)
 
     def cot_tx(m, j):
         d = to(j)
@@ -94,25 +99,75 @@
         f = fr(j)
         return same(g.at[m, rows(f), :], cot_sem, (m, j), f)
 
-    def ag_tx(m, j):
-        return same(A.at[m, :, col(me)], ag_sem, (m, j), mate_to(j))
-
-    def ag_rx(m, j):
-        f = mate_fr(j)
-        return same(A.at[m, :, col(f)], ag_sem, (m, j), f)
-
-    def ag_ptx(m):
-        return same(A.at[m, :, col(me)], ag_sem, (m, 0), partner)
-
-    def ag_prx(m):
-        return same(A.at[m, :, col(partner)], ag_sem, (m, 0), partner)
-
-    def ag_ftx(m, j):
-        return same(A.at[m, :, col(mate_fr(j))], ag_sem, (m, H + j), partner)
-
-    def ag_frx(m, j):
-        b = mate_fr(j) + 1 - 2 * par
-        return same(A.at[m, :, col(b)], ag_sem, (m, H + j), partner)
+    def cols_of(m, i):
+        return A.at[m, :, col(i)]
+
+    def rows_of(m, i):
+        return A.at[m, rows(i), :]
+
+    def ag_tx(blk, m, k):
+        return same(blk(m, me), ag_sem, (m, k), mate(k))
+
+    def ag_rx(blk, m, k):
+        return same(blk(m, mate(k)), ag_sem, (m, k), mate(k))
+
+    def ag_near(blk, m):
+        return same(blk(m, mate_of(near)), ag_sem, (m, near), mate_of(near))
+
+    def ag_far(blk, m):
+        return same(blk(m, mate_of(far)), ag_sem, (m, far), mate_of(far))
+
+    def ag_relay_tx(blk, m):
+        return same(blk(m, mate_of(near)), ag_sem, (m, 3), mate_of(far))
+
+    def ag_relay_rx(blk, m):
+        return same(blk(m, mate(3)), ag_sem, (m, 3), mate_of(far))
+
+    def ag_ptx(blk, m):
+        return same(blk(m, me), ag_sem, (m, 0), partner)
+
+    def ag_prx(blk, m):
+        return same(blk(m, partner), ag_sem, (m, 0), partner)
+
+    def ag_ftx(blk, m, k):
+        return same(blk(m, mate(k)), ag_sem, (m, H + k), partner)
+
+    def ag_ftx_of(blk, m, k):
+        return same(blk(m, mate_of(k)), ag_sem, (m, H + k), partner)
+
+    def ag_frx(blk, m, k):
+        return same(blk(m, mate(k) + 1 - 2 * par), ag_sem, (m, H + k), partner)
+
+    def gather_start(blk, m):
+        for k in direct:
+            ag_tx(blk, m, k).start()
+        ag_ptx(blk, m).start()
+
+    def gather_pass(blk, m):
+        if relayed:
+            ag_near(blk, m).wait_recv()
+            ag_relay_tx(blk, m).start()
+            ag_ftx_of(blk, m, near).start()
+            ag_far(blk, m).wait_recv()
+            ag_ftx_of(blk, m, far).start()
+        else:
+            for k in direct:
+                ag_rx(blk, m, k).wait_recv()
+                ag_ftx(blk, m, k).start()
+
+    def gather_last(blk, m):
+        if relayed:
+            ag_relay_rx(blk, m).wait_recv()
+            ag_ftx(blk, m, 3).start()
+
+    def gather_sent(blk, m):
+        for k in direct:
+            ag_tx(blk, m, k).wait_send()
+        ag_ptx(blk, m).wait_send()
+        if relayed:
+            ag_relay_tx(blk, m).wait_send()
+        for k in mates:
+            ag_ftx(blk, m, k).wait_send()
 
     def zf_tx(m):
         return cp(zout.at[m], A.at[m, :, col(me)], zf_sem, (m,), me, sec + 1)
@@ -146,11 +201,20 @@
     def p_rx(m, j):
         return same(prec.at[m, j], p_sem, (m, j), partner)
 
-    def q_tx(m, j):
-        return cp(qsend.at[m, j], qrec.at[m, j], q_sem, (m, j), mate_to(j))
-
-    def q_rx(m, j):
-        return same(qrec.at[m, j], q_sem, (m, j), mate_fr(j))
+    def q_tx(m, k):
+        return cp(qsend.at[m, k], qrec.at[m, k], q_sem, (m, k), mate(k))
+
+    def q_rx(m, k):
+        return same(qrec.at[m, k], q_sem, (m, k), mate(k))
+
+    def q_relay_tx(m):
+        return cp(qsend.at[m, 3], qrec.at[m, 3], q_sem, (m, 3), mate_of(near))
+
+    def q_relay_rx(m):
+        return same(qrec.at[m, 3], q_sem, (m, 3), mate_of(near))
+
+    def q_tx_of(m, k):
+        return cp(qsend.at[m, k], qrec.at[m, k], q_sem, (m, k), mate_of(k))
 
     def zb_tx(m):
         return cp(zg.at[m], g.at[m], zb_sem, (m,), me, sec - 1)
@@ -173,8 +237,6 @@
     def gg_rx(j):
         return same(ggr.at[j], gg_sem, (j,), fr(j))
 
-    others = range(1, S)
-    mates = range(1, H)
 
     barrier = pltpu.get_barrier_semaphore()
 
@@ -201,9 +263,8 @@
     def _():
         @pl.loop(0, M)
         def _(m):
-            for j in others:
-                in_tx(m, j).start()
-            A[m, rows(me), col(me)] = x_ref[m, :, col(me)]
+            A[m, rows(me), :] = x_ref[m]
+            gather_start(rows_of, m)
 
     @pl.when(is_last)
     def _():
@@ -221,48 +282,65 @@
         gain = to_col(gain_ref[:, col(b)])
         wp[col(b), :] = (w_ref[col(b), :].astype(F32) * gain * keep_of(b)).astype(BF16)
 
-    def gather_start(m):
-        for j in mates:
-            ag_tx(m, j).start()
-        ag_ptx(m).start()
-
-    @pl.when(is_first)
+    def add_block(carry, m, b):
+        acc, squares = carry
+        part = A[m, :, col(b)]
+        acc = acc + dot(part, wp[col(b), :], ((1,), (0,)))
+        wide = part.astype(F32)
+        return acc, squares + jnp.sum(wide * wide, axis=1, keepdims=True)
+
+    def zero():
+        return jnp.zeros((MB, C), F32), jnp.zeros((MB, 1), F32)
+
+    def keep_sums(m, carry):
+        raw[m] = carry[0]
+        inv_ref[m] = jnp.broadcast_to(lax.rsqrt(carry[1] / D + EPS), (MB, 128))
+
+    @pl.when(sec > 0)
     def _():
-        @pl.loop(0, M)
-        def _(m):
-            for j in others:
-                in_rx(m, j).wait_recv()
-            gather_start(m)
+        zf_rx(0).wait_recv()
+        gather_start(cols_of, 0)
 
     @pl.loop(0, M)
     def _(m):
+        @pl.when(is_first)
+        def _():
+            gather_pass(rows_of, m)
+            gather_last(rows_of, m)
+            ag_prx(rows_of, m).wait_recv()
+            for k in mates:
+                ag_frx(rows_of, m, k).wait_recv()
+            carry = zero()
+            for b in range(S):
+                carry = add_block(carry, m, b)
+            keep_sums(m, carry)
+
         @pl.when(sec > 0)
         def _():
-            zf_rx(m).wait_recv()
-            gather_start(m)
-
-        for j in mates:
-            ag_rx(m, j).wait_recv()
-            ag_ftx(m, j).start()
-        ag_prx(m).wait_recv()
-        for j in mates:
-            ag_frx(m, j).wait_recv()
-
-        @pl.when(sec > 0)
-        def _():
+            carry = add_block(zero(), m, me)
+            ag_prx(cols_of, m).wait_recv()
+            carry = add_block(carry, m, partner)
+            gather_pass(cols_of, m)
+            for k in direct:
+                carry = add_block(carry, m, mate(k))
+                ag_frx(cols_of, m, k).wait_recv()
+                carry = add_block(carry, m, mate(k) + 1 - 2 * par)
+            gather_last(cols_of, m)
+
+            @pl.when(m < M - 1)
+            def _():
+                zf_rx(m + 1).wait_recv()
+                gather_start(cols_of, m + 1)
+
+            if relayed:
+                carry = add_block(carry, m, mate(3))
+                ag_frx(cols_of, m, 3).wait_recv()
+                carry = add_block(carry, m, mate(3) + 1 - 2 * par)
+            keep_sums(m, carry)
             lo_tx(m).start()
 
-        acc = jnp.zeros((MB, C), F32)
-        squares = jnp.zeros((MB, 1), F32)
-        for b in range(S):
-            part = A[m, :, b * C:(b + 1) * C]
-            acc = acc + dot(part, wp[b * C:(b + 1) * C, :], ((1,), (0,)))
-            wide = part.astype(F32)
-            squares = squares + jnp.sum(wide * wide, axis=1, keepdims=True)
-        inv = lax.rsqrt(squares / D + EPS)
-        raw[m] = acc
-        inv_ref[m] = jnp.broadcast_to(inv, (MB, 128))
-        zout[m] = (A[m, :, col(me)].astype(F32) + inv * acc).astype(BF16)
+        inv = inv_ref[m][:, :1]
+        zout[m] = (A[m, :, col(me)].astype(F32) + inv * raw[m]).astype(BF16)
 
         @pl.when(sec < L - 1)
         def _():
@@ -287,8 +365,10 @@
         for j in others:
             gg_tx(j).start()
 
-    @pl.loop(0, M)
-    def _(m):
+    def partial_of(m, b):
+        return dot(g[m], wp[col(b), :], ((1,), (1,)))
+
+    def spread(m):
         @pl.when(is_last)
         def _():
             for j in others:
@@ -298,42 +378,52 @@
         def _():
             zb_rx(m).wait_recv()
 
-        def partial_of(b):
-            return dot(g[m], wp[col(b), :], ((1,), (1,)))
-
-        order = list(mates) + [0]
-        for j in order:
-            psend[m, j] = partial_of(((pair + j) % H) * 2 + 1 - par).astype(BF16)
-            p_tx(m, j).start()
-        inv = inv_ref[m][:, :1]
+        order = [3, 1, 2, 0] if relayed else list(mates) + [0]
+        for k in order:
+            psend[m, k] = partial_of(m, mate(k) + 1 - 2 * par).astype(BF16)
+            p_tx(m, k).start()
+
+        def chip_sum(k, b):
+            mine = partial_of(m, b)
+            p_rx(m, k).wait_recv()
+            return mine + prec[m, k].astype(F32)
+
+        if relayed:
+            qsend[m, 3] = chip_sum(3, mate(3)).astype(BF16)
+            q_relay_tx(m).start()
+            qsend[m, near] = chip_sum(near, mate_of(near)).astype(BF16)
+            q_tx_of(m, near).start()
+            last = chip_sum(far, mate_of(far))
+            q_relay_rx(m).wait_recv()
+            qsend[m, far] = (last + qrec[m, 3].astype(F32)).astype(BF16)
+            q_tx_of(m, far).start()
+        else:
+            for k in mates:
+                qsend[m, k] = chip_sum(k, mate(k)).astype(BF16)
+                q_tx(m, k).start()
         gv = g[m].astype(F32)
         nsend[m] = to_row(jnp.sum(gv * raw[m], axis=1, keepdims=True), 8)
         for j in others:
             n_tx(m, j).start()
-        gs[m] = (gv * inv).astype(BF16)
-        for j in mates:
-            mine = partial_of(mate_to(j))
-            p_rx(m, j).wait_recv()
-            qsend[m, j] = (mine + prec[m, j].astype(F32)).astype(BF16)
-            q_tx(m, j).start()
-        tot[...] = partial_of(me)
-
-        @pl.when(m == M - 1)
-        def _():
-            weight_grads()
-
-        p_rx(m, 0).wait_recv()
-        for j in mates:
-            q_rx(m, j).wait_recv()
+        gs[m] = (gv * inv_ref[m][:, :1]).astype(BF16)
+        tot[m] = chip_sum(0, me)
+
+    def lg_start(m):
+        for j in others:
+            lg_tx(m, j).start()
+
+    def finish(m):
+        scaled = tot[m]
+        for k in direct:
+            q_rx(m, k).wait_recv()
+            scaled = scaled + qrec[m, k].astype(F32)
         for j in others:
             n_rx(m, j).wait_recv()
-        scaled = tot[...] + prec[m, 0].astype(F32)
-        for j in mates:
-            scaled = scaled + qrec[m, j].astype(F32)
         sums = nsend[m]
         for j in others:
             sums = sums + nrec[m, j]
         inner = to_col(sums[:1]) / D
+        inv = inv_ref[m][:, :1]
         grad = (
             g[m].astype(F32)
             + inv * scaled
@@ -345,9 +435,31 @@
         def _():
             zb_tx(m).start()
 
-        for j in others:
-            lg_tx(m, j).start()
+        @pl.when(is_first)
+        def _():
+            lg_start(m)
+
         lg_ref[m, :, col(me)] = zg[m, rows(me), :]
+
+    @pl.loop(0, M + 1)
+    def _(i):
+        @pl.when(i < M)
+        def _():
+            spread(i)
+
+        @pl.when(i == M)
+        def _():
+            weight_grads()
+
+        @pl.when(i > 0)
+        def _():
+            finish(i - 1)
+
+    @pl.when(sec > 0)
+    def _():
+        @pl.loop(0, M)
+        def _(m):
+            lg_start(m)
 
     for j in others:
         gg_rx(j).wait_recv()
@@ -363,8 +475,11 @@
     def _(m):
         @pl.when(is_first)
         def _():
-            for j in others:
-                in_tx(m, j).wait_send()
+            gather_sent(rows_of, m)
+
+        @pl.when(sec > 0)
+        def _():
+            gather_sent(cols_of, m)
 
         @pl.when(is_last)
         def _():
@@ -383,11 +498,8 @@
             lo_tx(m).wait_send()
             zb_tx(m).wait_send()
 
-        for j in mates:
-            ag_tx(m, j).wait_send()
-            ag_ftx(m, j).wait_send()
-            q_tx(m, j).wait_send()
-        ag_ptx(m).wait_send()
+        for k in mates:
+            q_tx(m, k).wait_send()
         for j in range(H):
             p_tx(m, j).wait_send()
         for j in others:
@@ -426,7 +538,7 @@
             pltpu.VMEM((M, MB, C), BF16),
             pltpu.VMEM((M, MB, C), BF16),
             pltpu.VMEM((M, MB, C), BF16),
-            pltpu.VMEM((MB, C), F32),
+            pltpu.VMEM((M, MB, C), F32),
             pltpu.VMEM((M, H, MB, C), BF16),
             pltpu.VMEM((M, H, MB, C), BF16),
             pltpu.VMEM((M, H, MB, C), BF16),
@@ -435,7 +547,6 @@
             pltpu.VMEM((M, S, 8, MB), F32),
             pltpu.VMEM((S, 8, C), F32),
             pltpu.VMEM((S, 8, C), F32),
-            dma((2, M, S)),
             dma((2, M, S)),
             dma((2, M, S)),
             dma((2, M, S)),

time: 206 us -> 200 us (0.971)
  Pallas kernels: 194 us -> 188 us
    pallas_call x1, Pallas kernels: 194 us -> 188 us  [local(): pl.pallas_call(functools.partial(kernel, L, S, M, block), out_shape=(jax....]
where the time goes in v1:
time: 200 us; the launch traced here: 199 us
  Pallas kernels  188 us (94%)
  local copies, waits for them, and re-layouts  9.77 us (5%)
    pallas_call x1, Pallas kernels, local(): pl.pallas_call(functools.partial(kernel, L, S, M, block), out_shape=(jax....  188 us
    unnamed x6, local copies, waits for them, and re-layouts  8.79 us

profile of v1, /device:TPU:0, one launch (start us, length us, event | category | flops | bytes accessed | tf_op | source)
XLA Modules:
  0.0 199.4 jit_solution(5535996427554784565)
XLA Ops:
  0.6 0.7 convert_bitcast_fusion
  1.3 0.1 copy.9
  1.4 0.1 broadcast_in_dim.6
  1.5 0.8 reshape_reshape.3.keep_ref
  2.3 188.3 %shard_map.84 = (bf16[4,16,4096]{2,1,0:T(8,128)(2,1)}, bf16[4,16,4096]{2,1,0:T(8,128)(2,1)}, bf16[4096,512]{1,0:T(8,128)(2,1)}, f32[1,512]{1,0:T(1,128)}) custom-call(bf16[4,16,4096]{2,1,0:T(8,128)(2,1)} %bitcast.12, f32[1,4096]{1,0:T(1,128)} %gain_ref.1, bf16[4096,512]{1,0:T(8,128)(2,1)} %bitcast.11, f32[8,8,512]{2,1,0:T(8,128)} %reshape_reshape.3.keep_ref, ...), custom_call_target="tpu_custom_call" | custom-call | flops 6442450944 | bytes 25165824 | tf_op jit(solution)/shard_map/pallas_call | solution.py:522
  190.6 1.9 copy.14
  192.5 1.9 copy.15
  194.3 0.0 copy-start
  194.3 4.5 %copy.16 = bf16[1,4096,512]{2,1,0:T(8,128)(2,1)} copy(bf16[1,4096,512]{2,1,0:T(8,128)(2,1)} %bitcast.8) | data formatting | bytes 8388608
  198.8 0.0 copy-done
  198.8 0.6 copy.17
Async XLA Ops:
  194.3 4.5 %copy-start = (f32[1,512]{1,0:T(1,128)S(1)}, f32[1,512]{1,0:T(1,128)}, u32[]{:S(2)}) copy-start(f32[1,512]{1,0:T(1,128)} %get-tuple-element.19) | copy-start | bytes 6148
